TPU v7x, 32 devices: a whole 2x2x4 slice. The times are simulated.
32 devices in a mesh: grid: 8 (over z, core), band: 4 (over y, x).
Axes of the slice: x: 2, y: 2, z: 4, core: 2. Of those that a mesh axis runs over, the one named last changes fastest.
Arguments:
- orbitals: float32 [2048, 8192], P('band', 'grid'), may hold values from -0.6 to 0.6
- points: int32 [1536], replicated, may hold values from 0 to 8191, as said below
Outputs:
- fitted: float32 [8192, 1536], P(('grid', 'band'))
Inputs may be any that keep to these rules, and one draw needn't show every extreme that they name: Grid indices of interpolation points; each aligned domain of grid points d * 1024 to (d + 1) * 1024 - 1 holds at least one, the rest cluster unevenly around a few centres; repeats may occur.
All inputs are finite; a program needn't handle non-finite values.
Results may differ from a plain program's by a relative error of at most 0.000092.
Values sent between devices are 32-bit elements; how exact they have to be, the bound alone decides.
A program may use at most 64 MiB of HBM per device.

v0:
```python
import jax
import jax.numpy as jnp
from jax import lax
from jax.sharding import PartitionSpec as P


def contract(block, sampled):
    return lax.dot_general(
        block,
        sampled,
        (((0,), (0,)), ((), ())),
        precision=lax.Precision.HIGHEST,
        preferred_element_type=jnp.float32,
    )


def shards(orbitals, points):
    slab = orbitals.shape[1]
    offset = lax.axis_index("grid") * slab
    local = points - offset
    inside = (local >= 0) & (local < slab)
    safe_idx = jnp.clip(local, 0, slab - 1)
    picked = jnp.take(orbitals, safe_idx, axis=1) * inside[None, :].astype(jnp.float32)
    sampled = lax.psum(picked, "grid")
    density = contract(orbitals, sampled)
    share = lax.psum_scatter(density, "band", scatter_dimension=1, tiled=True)
    squared = share * share
    return lax.all_to_all(squared, "band", split_axis=0, concat_axis=1, tiled=True)


def solution(mesh):
    in_specs = (P("band", "grid"), P())
    out_specs = P(("grid", "band"), None)
    return jax.shard_map(shards, mesh=mesh, in_specs=in_specs, out_specs=out_specs, check_vma=False)
```

profile of v0, /device:TPU:0, one launch (start us, length us, event | category | flops | bytes accessed | tf_op | source)
XLA Modules:
  0.0 214.6 jit_solution(8979033957454680582)
XLA Ops:
  6.5 0.0 all-reduce.2.cloned.1.call-start
  6.5 0.7 compare_and_fusion
  7.3 1.9 copy.5
  9.2 4.9 %gather_fusion = f32[1536,512]{1,0:T(8,128)} fusion(f32[512,1024]{0,1:T(8,128)S(1)} %copy.5, s32[2048]{0:T(1024)S(1)} %pad_clamp_fusion), kind=kCustom, calls=%fused_computation | custom fusion | bytes 6297600 | tf_op jit(solution)/shard_map/jit(_take)/gather | solution.py:23
  14.1 3.6 %multiply_bitcast_fusion = f32[512,1536]{0,1:T(8,128)} fusion(f32[1536,512]{1,0:T(8,128)} %gather_fusion, f32[1536]{0:T(1024)S(1)} %get-tuple-element.7, pred[1536]{0:T(1024)(128)(4,1)S(1)} %get-tuple-element.5), kind=kLoop, calls=%fused_computation.2 | loop fusion | flops 1572864 | bytes 6299136 | tf_op jit(solution)/shard_map/mul | solution.py:23
  17.8 0.0 copy-start
  17.8 0.0 all-reduce.2.cloned.1.call-update
  17.8 0.0 reduce-scatter.2.cloned.1.call-start
  17.8 79.7 %all-reduce.2.cloned.1.call-done = f32[512,1536]{0,1:T(8,128)} async-done(((f32[512,1536]{0,1:T(8,128)}), f32[512,1536]{0,1:T(8,128)}) %all-reduce.2.cloned.1.call-update) | async-done | bytes 3145744 | tf_op jit(solution)/shard_map/psum | solution.py:24
  97.6 0.0 copy-done
  97.6 13.5 %convolution_bitcast_fusion = f32[1024,1536]{0,1:T(8,128)} fusion(f32[512,1536]{0,1:T(8,128)} %all-reduce.2.cloned.1.call-done, f32[512,1024]{1,0:T(8,128)S(1)} %copy-done), kind=kOutput, calls=%fused_computation.1 | convolution fusion | flops 9663676416 | bytes 11534336 | tf_op jit(solution)/shard_map/dot_general | solution.py:8
  111.0 0.0 reduce-scatter.2.cloned.1.call-update
  111.1 70.2 %reduce-scatter.2.cloned.1.call-done = f32[1024,384]{0,1:T(8,128)} async-done(((f32[1024,1536]{0,1:T(8,128)}), f32[1024,384]{0,1:T(8,128)}) %reduce-scatter.2.cloned.1.call-update) | async-done | bytes 1572880 | tf_op jit(solution)/shard_map/reduce_scatter | solution.py:26
  181.3 2.2 %mul.17 = f32[1024,384]{0,1:T(8,128)S(1)} multiply(f32[1024,384]{0,1:T(8,128)} %reduce-scatter.2.cloned.1.call-done, f32[1024,384]{0,1:T(8,128)} %reduce-scatter.2.cloned.1.call-done) | non-fusion elementwise | flops 393216 | bytes 4718592 | tf_op jit(solution)/shard_map/mul | solution.py:27
  183.5 0.1 copy.10
  183.6 22.5 %all_to_all.19 = f32[4,256,384]{1,2,0:T(8,128)S(1)} all-to-all(f32[4,256,384]{1,2,0:T(8,128)S(1)} %bitcast.13), channel_id=1, replica_groups=mesh['grid'=8,'band'=4] {'band'}, dimensions={0} | all-to-all | bytes 3145728 | tf_op jit(solution)/shard_map/all_to_all | solution.py:28
  206.1 1.6 copy.7
  (1 shorter events, 0.0 us)
Async XLA Ops:
  6.5 91.0 %all-reduce.2.cloned.1.call-start = ((), (), s32[]{:S(2)}) async-start(), calls=%async_computation.2 | async-start | bytes 6291456 | tf_op jit(solution)/shard_map/psum | solution.py:24
  17.8 79.8 %copy-start = (f32[512,1024]{1,0:T(8,128)S(1)}, f32[512,1024]{1,0:T(8,128)}, u32[]{:S(2)}) copy-start(f32[512,1024]{1,0:T(8,128)} %param.2) | copy-start | bytes 6291460
  17.8 163.5 %reduce-scatter.2.cloned.1.call-start = ((), (), s32[]{:S(2)}) async-start(), calls=%async_computation.3 | async-start | bytes 7864320 | tf_op jit(solution)/shard_map/reduce_scatter | solution.py:26
Sparse Core Ops, SparseCore 0:
  17.9 79.6 all-reduce.1
  111.2 70.0 reduce-scatter.1
where the time goes:
time: 215 us
  waiting for transfers between devices  150 us (70%)
  blocking collectives  22.5 us (10%)
  matrix products  13.5 us (6%)
  between operations  13.4 us (6%)
  local copies, waits for them, and re-layouts  8.59 us (4%)
  other arithmetic  6.58 us (3%)
    psum x1, waiting for transfers between devices, shards(): sampled = lax.psum(picked, 'grid')  79.7 us
    reduce_scatter x1, waiting for transfers between devices, shards(): share = lax.psum_scatter(density, 'band', scatter_dimension=1, tiled=True)  70.2 us
    all_to_all x1, blocking collectives, shards(): lax.all_to_all(squared, 'band', split_axis=0, concat_axis=1, tiled=True)  22.5 us
    dot_general x1, matrix products, contract(): lax.dot_general(block, sampled, (((0,), (0,)), ((), ())), precision=lax.P...  13.5 us
    gather x1, local copies, waits for them, and re-layouts, shards(): jnp.take(orbitals, safe_idx, axis=1) * inside[None, :].astype(jnp.float32)  4.93 us
  transfers between devices with their start and end apart: 2, of which 2 were waited for; matrix products, arithmetic and copies ran while one was open for 0% of the time, Pallas kernels for 0%

commit v1 on v0

v1 whole, which is shorter than its diff:
```python
import functools

import jax
import jax.numpy as jnp
from jax import lax
from jax.experimental import pallas as pl
from jax.experimental.pallas import tpu as pltpu
from jax.sharding import PartitionSpec as P

WIDTH = 128


def split(x):
    high = x.astype(jnp.bfloat16)
    return high, (x - high.astype(jnp.float32)).astype(jnp.bfloat16)


def dot(a, b):
    return lax.dot_general(a, b, (((1,), (0,)), ((), ())), preferred_element_type=jnp.float32)


def kernel(
    chips, group, bits,
    orb_ref, pts_ref, out_ref,
    halves, turned, turned_hi, turned_lo,
    own, sibs, came, incl, sib_incl, acc, *rest,
):
    got, sems = rest[:bits], rest[bits:]
    own_s, own_r, came_s, came_r, incl_s, incl_r, red_s, red_r = sems
    bands, slab = orb_ref.shape
    chunks = pts_ref.shape[0]
    rows = slab // group
    g, b = lax.axis_index("grid"), lax.axis_index("band")
    z, core = g // 2, g % 2
    toward = 1 - 2 * core
    pos = z * (1 - core) + (chips - 1 - z) * core
    sibling = g + toward
    after, before = g + 2 * toward, g - 2 * toward
    first, last = pos == 0, pos == chips - 1
    flip = [(1 - 2 * ((b // 2**k) % 2)) * 2**k for k in range(bits)]

    def partner(chunk, stage):
        k = (chunk + stage) % bits
        return b + sum((k == i).astype(jnp.int32) * flip[i] for i in range(bits))

    barrier = pltpu.get_barrier_semaphore()

    def greet(to_g, to_b):
        pl.semaphore_signal(barrier, inc=1, device_id=(to_g, to_b), device_id_type=pl.DeviceIdType.MESH)

    greet(sibling, b)
    for k in range(bits):
        greet(g, b + flip[k])

    @pl.when(pos > 0)
    def _():
        greet(before, b)

    @pl.when(pos < chips - 1)
    def _():
        greet(after, b)

    def remote(src, dst, send, recv, to_g, to_b):
        return pltpu.make_async_remote_copy(
            src_ref=src, dst_ref=dst, send_sem=send, recv_sem=recv,
            device_id=(to_g, to_b), device_id_type=pl.DeviceIdType.MESH,
        )

    def own_copy(t):
        return remote(own.at[t], sibs.at[t], own_s.at[t], own_r.at[t], sibling, b)

    def chain_copy(t):
        return remote(incl.at[t], came.at[t], came_s.at[t], came_r.at[t], after, b)

    def incl_copy(t):
        return remote(incl.at[t], sib_incl.at[t], incl_s.at[t], incl_r.at[t], sibling, b)

    def reduce_copy(t, stage):
        size = slab >> (stage + 1)
        return remote(
            acc.at[t, pl.ds(size, size)], got[stage].at[t],
            red_s.at[stage, t], red_r.at[stage, t], g, partner(t, stage),
        )

    def pick(t):
        where = pts_ref[t] - g * slab
        hot = lax.broadcasted_iota(jnp.int32, (slab, WIDTH), 0) == where
        both = dot(halves[...], jnp.where(hot, 1.0, 0.0).astype(jnp.bfloat16))
        own[t] = both[:bands] + both[bands:]

    def turn():
        turned[...] = orb_ref[...].T
        for turn_by in range(bits):
            for slot in range(group):
                block = b
                for j in range(bits):
                    if slot & (group >> (j + 1)):
                        block = block + flip[(turn_by + j) % bits]
                high, low = split(turned[pl.ds(pl.multiple_of(block * rows, rows), rows), :])
                turned_hi[turn_by, slot * rows:(slot + 1) * rows, :] = high
                turned_lo[turn_by, slot * rows:(slot + 1) * rows, :] = low

    def forward(t):
        own_copy(t).wait_recv()

        @pl.when(first)
        def _():
            came[t] = jnp.zeros((bands, WIDTH), jnp.float32)

        @pl.when(jnp.logical_not(first))
        def _():
            chain_copy(t).wait_recv()

        incl[t] = came[t] + own[t] + sibs[t]

        @pl.when(jnp.logical_not(last))
        def _():
            chain_copy(t).start()

        incl_copy(t).start()

    def contract(t):
        incl_copy(t).wait_recv()
        high, low = split(came[t] + sib_incl[t])
        pair = jnp.concatenate([high, low], axis=1)
        by = t % bits
        half = slab // 2

        def part(at):
            two = dot(turned_hi[by, at:at + half, :], pair)
            acc[t, at:at + half, :] = two[:, :WIDTH] + two[:, WIDTH:] + dot(turned_lo[by, at:at + half, :], high)

        part(half)
        reduce_copy(t, 0).start()
        part(0)

    def add(t, stage):
        size = slab >> (stage + 1)
        reduce_copy(t, stage).wait_recv()
        if stage + 1 < bits:
            less = size // 2
            acc[t, less:size, :] += got[stage][t, less:, :]
            reduce_copy(t, stage + 1).start()
            acc[t, :less, :] += got[stage][t, :less, :]
        else:
            out_ref[:, pl.ds(pl.multiple_of(t * WIDTH, WIDTH), WIDTH)] = acc[t, :size, :] + got[stage][t]

    high, low = split(orb_ref[...])
    halves[:bands, :] = high
    halves[bands:, :] = low
    pick(0)
    pl.semaphore_wait(barrier, 1 + bits + (pos > 0).astype(jnp.int32) + (pos < chips - 1).astype(jnp.int32))
    own_copy(0).start()

    behind = chips - 1

    def step(s, carry):
        @pl.when(s + 1 < chunks)
        def _():
            pick(s + 1)
            own_copy(s + 1).start()

        f = s - pos

        @pl.when(jnp.logical_and(f >= 0, f < chunks))
        def _():
            forward(f)

        @pl.when(s == 0)
        def _():
            turn()

        c = s - behind

        @pl.when(jnp.logical_and(c >= 0, c < chunks))
        def _():
            contract(c)

        for stage in range(bits):
            r = c - 2 * (stage + 1)

            @pl.when(jnp.logical_and(r >= 0, r < chunks))
            def _(r=r, stage=stage):
                add(r, stage)

        return carry

    lax.fori_loop(0, chunks + behind + 2 * bits, step, 0)

    def drain(t, carry):
        own_copy(t).wait_send()

        @pl.when(jnp.logical_not(last))
        def _():
            chain_copy(t).wait_send()

        incl_copy(t).wait_send()
        for stage in range(bits):
            reduce_copy(t, stage).wait_send()
        return carry

    lax.fori_loop(0, chunks, drain, 0)


def shards(sizes, orbitals, points):
    grid, group = sizes
    bits = group.bit_length() - 1
    bands, slab = orbitals.shape
    columns = points.shape[0]
    chunks = columns // WIDTH
    rows = slab // group
    piece = (chunks, bands, WIDTH)
    dma = pltpu.SemaphoreType.DMA
    density = pl.pallas_call(
        functools.partial(kernel, grid // 2, group, bits),
        out_shape=jax.ShapeDtypeStruct((rows, columns), jnp.float32),
        in_specs=[pl.BlockSpec(memory_space=pltpu.VMEM)] * 2,
        out_specs=pl.BlockSpec(memory_space=pltpu.VMEM),
        scratch_shapes=[
            pltpu.VMEM((2 * bands, slab), jnp.bfloat16),
            pltpu.VMEM((slab, bands), jnp.float32),
            pltpu.VMEM((bits, slab, bands), jnp.bfloat16),
            pltpu.VMEM((bits, slab, bands), jnp.bfloat16),
            *[pltpu.VMEM(piece, jnp.float32) for _ in range(5)],
            pltpu.VMEM((chunks, slab, WIDTH), jnp.float32),
            *[pltpu.VMEM((chunks, slab >> (j + 1), WIDTH), jnp.float32) for j in range(bits)],
            *[dma((chunks,)) for _ in range(6)],
            dma((bits, chunks)),
            dma((bits, chunks)),
        ],
        compiler_params=pltpu.CompilerParams(
            collective_id=0, has_side_effects=True, vmem_limit_bytes=60 * 2**20
        ),
        cost_estimate=pl.CostEstimate(
            flops=10 * bands * slab * columns, bytes_accessed=8 * bands * slab, transcendentals=0
        ),
    )(orbitals, points.reshape(chunks, 1, WIDTH))
    return density * density


def solution(mesh):
    sizes = (mesh.shape["grid"], mesh.shape["band"])
    return jax.shard_map(
        functools.partial(shards, sizes),
        mesh=mesh,
        in_specs=(P("band", "grid"), P()),
        out_specs=P(("grid", "band"), None),
        check_vma=False,
    )
```

time: 215 us -> 90.5 us (0.42)
  waiting for transfers between devices: 150 us -> 0 us
  Pallas kernels: 0 us -> 85.7 us
  blocking collectives: 22.5 us -> 0 us
  matrix products: 13.5 us -> 0 us
  between operations: 13.4 us -> 0.01 us
  local copies, waits for them, and re-layouts: 8.59 us -> 1.3 us
  other arithmetic: 6.58 us -> 3.24 us
    pallas_call x0 -> x1, Pallas kernels: none -> 85.7 us  [shards(): pl.pallas_call(functools.partial(kernel, grid // 2, group, bits), out_sha...]
    psum x1 -> x0, waiting for transfers between devices: 79.7 us -> none  [shards(): sampled = lax.psum(picked, 'grid')]
    reduce_scatter x1 -> x0, waiting for transfers between devices: 70.2 us -> none  [shards(): share = lax.psum_scatter(density, 'band', scatter_dimension=1, tiled=True)]
    all_to_all x1 -> x0, blocking collectives: 22.5 us -> none  [shards(): lax.all_to_all(squared, 'band', split_axis=0, concat_axis=1, tiled=True)]
    dot_general x1 -> x0, matrix products: 13.5 us -> none  [contract(): lax.dot_general(block, sampled, (((0,), (0,)), ((), ())), precision=lax.P...]
    gather x1 -> x0, local copies, waits for them, and re-layouts: 4.93 us -> none  [shards(): jnp.take(orbitals, safe_idx, axis=1) * inside[None, :].astype(jnp.float32)]
    mul x2 -> x1, other arithmetic: 5.87 us -> 3.24 us  [shards(): return density * density]
  transfers between devices with their start and end apart: 2 -> 0, of which waited for: 2 -> 0; matrix products, arithmetic and copies ran while one was open for 0% -> 0% of each run, Pallas kernels for 0% -> 0%
where the time goes in v1:
time: 90.5 us; the launch traced here: 90.3 us
  Pallas kernels  85.7 us (95%)
  other arithmetic  3.24 us (4%)
  local copies, waits for them, and re-layouts  1.3 us (1%)
    pallas_call x1, Pallas kernels, shards(): pl.pallas_call(functools.partial(kernel, grid // 2, group, bits), out_sha...  85.7 us
    mul x1, other arithmetic, shards(): return density * density  3.24 us

profile of v1, /device:TPU:0, one launch (start us, length us, event | category | flops | bytes accessed | tf_op | source)
XLA Modules:
  0.0 90.3 jit_solution(6407237895218840432)
XLA Ops:
  0.0 1.3 %reshape.3.pts_ref = s32[12,1,128]{2,1,0:T(1,128)} reshape(s32[1536]{0:T(1024)} %param.3) | data formatting | bytes 12288 | tf_op jit(solution)/shard_map/reshape | solution.py:237
  1.3 85.7 %shard_map.28 = f32[256,1536]{1,0:T(8,128)} custom-call(f32[512,1024]{1,0:T(8,128)} %orb_ref.1, s32[12,1,128]{2,1,0:T(1,128)} %reshape.3.pts_ref), custom_call_target="tpu_custom_call" | custom-call | flops 8053063680 | bytes 4194304 | tf_op jit(solution)/shard_map/pallas_call | solution.py:214
  87.0 3.2 %mul.3 = f32[256,1536]{1,0:T(8,128)} multiply(f32[256,1536]{1,0:T(8,128)} %shard_map.28, f32[256,1536]{1,0:T(8,128)} %shard_map.28) | non-fusion elementwise | flops 393216 | bytes 4718592 | tf_op jit(solution)/shard_map/mul | solution.py:238

commit v2 on v1

--- a/solution.py
+++ b/solution.py
@@ -8,6 +8,8 @@
 from jax.sharding import PartitionSpec as P
 
 WIDTH = 128
+PIECES = 4
+LAG = 2
 
 
 def split(x):
@@ -28,7 +30,7 @@
     got, sems = rest[:bits], rest[bits:]
     own_s, own_r, came_s, came_r, incl_s, incl_r, red_s, red_r = sems
     bands, slab = orb_ref.shape
-    chunks = pts_ref.shape[0]
+    chunks = pts_ref.shape[0] // WIDTH
     rows = slab // group
     g, b = lax.axis_index("grid"), lax.axis_index("band")
     z, core = g // 2, g % 2
@@ -40,7 +42,7 @@
     flip = [(1 - 2 * ((b // 2**k) % 2)) * 2**k for k in range(bits)]
 
     def partner(chunk, stage):
-        k = (chunk + stage) % bits
+        k = (chunk + core + stage) % bits
         return b + sum((k == i).astype(jnp.int32) * flip[i] for i in range(bits))
 
     barrier = pltpu.get_barrier_semaphore()
@@ -69,21 +71,27 @@
     def own_copy(t):
         return remote(own.at[t], sibs.at[t], own_s.at[t], own_r.at[t], sibling, b)
 
-    def chain_copy(t):
-        return remote(incl.at[t], came.at[t], came_s.at[t], came_r.at[t], after, b)
+    def chain_copy(t, p):
+        size = bands // PIECES
+        at = pl.ds(p * size, size)
+        return remote(incl.at[t, at], came.at[t, at], came_s.at[p, t], came_r.at[p, t], after, b)
 
     def incl_copy(t):
         return remote(incl.at[t], sib_incl.at[t], incl_s.at[t], incl_r.at[t], sibling, b)
 
-    def reduce_copy(t, stage):
+    def parts(stage):
+        return (1, 0) if stage + 1 < bits else (0,)
+
+    def reduce_copy(t, stage, part):
         size = slab >> (stage + 1)
+        each = size // len(parts(stage))
         return remote(
-            acc.at[t, pl.ds(size, size)], got[stage].at[t],
-            red_s.at[stage, t], red_r.at[stage, t], g, partner(t, stage),
+            acc.at[t, pl.ds(size + part * each, each)], got[stage].at[t, pl.ds(part * each, each)],
+            red_s.at[stage, part, t], red_r.at[stage, part, t], g, partner(t, stage),
         )
 
     def pick(t):
-        where = pts_ref[t] - g * slab
+        where = (pts_ref[pl.ds(pl.multiple_of(t * WIDTH, WIDTH), WIDTH)] - g * slab)[None, :]
         hot = lax.broadcasted_iota(jnp.int32, (slab, WIDTH), 0) == where
         both = dot(halves[...], jnp.where(hot, 1.0, 0.0).astype(jnp.bfloat16))
         own[t] = both[:bands] + both[bands:]
@@ -107,15 +115,19 @@
         def _():
             came[t] = jnp.zeros((bands, WIDTH), jnp.float32)
 
-        @pl.when(jnp.logical_not(first))
-        def _():
-            chain_copy(t).wait_recv()
-
-        incl[t] = came[t] + own[t] + sibs[t]
-
-        @pl.when(jnp.logical_not(last))
-        def _():
-            chain_copy(t).start()
+        for p in range(PIECES):
+            size = bands // PIECES
+            at = pl.ds(p * size, size)
+
+            @pl.when(jnp.logical_not(first))
+            def _(p=p):
+                chain_copy(t, p).wait_recv()
+
+            incl[t, at] = came[t, at] + own[t, at] + sibs[t, at]
+
+            @pl.when(jnp.logical_not(last))
+            def _(p=p):
+                chain_copy(t, p).start()
 
         incl_copy(t).start()
 
@@ -123,7 +135,7 @@
         incl_copy(t).wait_recv()
         high, low = split(came[t] + sib_incl[t])
         pair = jnp.concatenate([high, low], axis=1)
-        by = t % bits
+        by = (t + core) % bits
         half = slab // 2
 
         def part(at):
@@ -131,18 +143,23 @@
             acc[t, at:at + half, :] = two[:, :WIDTH] + two[:, WIDTH:] + dot(turned_lo[by, at:at + half, :], high)
 
         part(half)
-        reduce_copy(t, 0).start()
+        for p in parts(0):
+            reduce_copy(t, 0, p).start()
         part(0)
 
     def add(t, stage):
         size = slab >> (stage + 1)
-        reduce_copy(t, stage).wait_recv()
+        if stage > 0:
+            reduce_copy(t, stage - 1, 0).wait_recv()
+            acc[t, :size, :] += got[stage - 1][t, :size, :]
         if stage + 1 < bits:
             less = size // 2
+            reduce_copy(t, stage, 1).wait_recv()
             acc[t, less:size, :] += got[stage][t, less:, :]
-            reduce_copy(t, stage + 1).start()
-            acc[t, :less, :] += got[stage][t, :less, :]
+            for p in parts(stage + 1):
+                reduce_copy(t, stage + 1, p).start()
         else:
+            reduce_copy(t, stage, 0).wait_recv()
             out_ref[:, pl.ds(pl.multiple_of(t * WIDTH, WIDTH), WIDTH)] = acc[t, :size, :] + got[stage][t]
 
     high, low = split(orb_ref[...])
@@ -177,7 +194,7 @@
             contract(c)
 
         for stage in range(bits):
-            r = c - 2 * (stage + 1)
+            r = c - LAG * (stage + 1)
 
             @pl.when(jnp.logical_and(r >= 0, r < chunks))
             def _(r=r, stage=stage):
@@ -185,18 +202,20 @@
 
         return carry
 
-    lax.fori_loop(0, chunks + behind + 2 * bits, step, 0)
+    lax.fori_loop(0, chunks + behind + LAG * bits, step, 0)
 
     def drain(t, carry):
         own_copy(t).wait_send()
 
         @pl.when(jnp.logical_not(last))
         def _():
-            chain_copy(t).wait_send()
+            for p in range(PIECES):
+                chain_copy(t, p).wait_send()
 
         incl_copy(t).wait_send()
         for stage in range(bits):
-            reduce_copy(t, stage).wait_send()
+            for p in parts(stage):
+                reduce_copy(t, stage, p).wait_send()
         return carry
 
     lax.fori_loop(0, chunks, drain, 0)
@@ -224,17 +243,22 @@
             *[pltpu.VMEM(piece, jnp.float32) for _ in range(5)],
             pltpu.VMEM((chunks, slab, WIDTH), jnp.float32),
             *[pltpu.VMEM((chunks, slab >> (j + 1), WIDTH), jnp.float32) for j in range(bits)],
-            *[dma((chunks,)) for _ in range(6)],
-            dma((bits, chunks)),
-            dma((bits, chunks)),
+            dma((chunks,)),
+            dma((chunks,)),
+            dma((PIECES, chunks)),
+            dma((PIECES, chunks)),
+            dma((chunks,)),
+            dma((chunks,)),
+            dma((bits, 2, chunks)),
+            dma((bits, 2, chunks)),
         ],
         compiler_params=pltpu.CompilerParams(
-            collective_id=0, has_side_effects=True, vmem_limit_bytes=60 * 2**20
+            collective_id=0, has_side_effects=True, vmem_limit_bytes=44 * 2**20
         ),
         cost_estimate=pl.CostEstimate(
             flops=10 * bands * slab * columns, bytes_accessed=8 * bands * slab, transcendentals=0
         ),
-    )(orbitals, points.reshape(chunks, 1, WIDTH))
+    )(orbitals, points)
     return density * density
 
 

time: 90.5 us -> 77.5 us (0.86)
  Pallas kernels: 85.7 us -> 73.6 us
  other arithmetic: 3.24 us -> 1.34 us
  local copies, waits for them, and re-layouts: 1.3 us -> 2.29 us
    pallas_call x1, Pallas kernels: 85.7 us -> 73.6 us  [shards(): pl.pallas_call(functools.partial(kernel, grid // 2, group, bits), out_sha...]
    unnamed x0 -> x4, local copies, waits for them, and re-layouts: none -> 2.29 us
    mul x1, other arithmetic: 3.24 us -> 1.34 us  [shards(): return density * density]
    reshape x1 -> x0, local copies, waits for them, and re-layouts: 1.3 us -> none  [shards(): points.reshape(chunks, 1, WIDTH)]
where the time goes in v2:
time: 77.5 us; the launch traced here: 77.3 us
  Pallas kernels  73.6 us (95%)
  local copies, waits for them, and re-layouts  2.29 us (3%)
  other arithmetic  1.34 us (2%)
    pallas_call x1, Pallas kernels, shards(): pl.pallas_call(functools.partial(kernel, grid // 2, group, bits), out_sha...  73.6 us
    unnamed x4, local copies, waits for them, and re-layouts  2.29 us

profile of v2, /device:TPU:0, one launch (start us, length us, event | category | flops | bytes accessed | tf_op | source)
XLA Modules:
  0.0 77.3 jit_solution(13555032699897062907)
XLA Ops:
  0.0 0.0 copy-start
  0.0 1.6 %copy-done = f32[512,1024]{1,0:T(8,128)S(1)} copy-done((f32[512,1024]{1,0:T(8,128)S(1)}, f32[512,1024]{1,0:T(8,128)}, u32[]{:S(2)}) %copy-start) | copy-done | bytes 2097176
  1.6 0.0 copy-start.1
  1.6 0.7 copy-done.1
  2.3 73.6 %shard_map.28 = f32[256,1536]{1,0:T(8,128)S(1)} custom-call(f32[512,1024]{1,0:T(8,128)S(1)} %copy-done, s32[1536]{0:T(1024)S(1)} %copy-done.1), custom_call_target="tpu_custom_call" | custom-call | flops 8053063680 | bytes 4194304 | tf_op jit(solution)/shard_map/pallas_call | solution.py:233
  75.9 1.3 %mul.3 = f32[256,1536]{1,0:T(8,128)} multiply(f32[256,1536]{1,0:T(8,128)S(1)} %shard_map.28, f32[256,1536]{1,0:T(8,128)S(1)} %shard_map.28) | non-fusion elementwise | flops 393216 | bytes 4718592 | tf_op jit(solution)/shard_map/mul | solution.py:262
Async XLA Ops:
  0.0 1.6 %copy-start = (f32[512,1024]{1,0:T(8,128)S(1)}, f32[512,1024]{1,0:T(8,128)}, u32[]{:S(2)}) copy-start(f32[512,1024]{1,0:T(8,128)} %orb_ref.1) | copy-start | bytes 6291460
  1.6 0.7 copy-start.1

commit v3 on v2

--- a/solution.py
+++ b/solution.py
@@ -10,6 +10,7 @@
 WIDTH = 128
 PIECES = 4
 LAG = 2
+REST = 2
 
 
 def split(x):
@@ -194,7 +195,7 @@
             contract(c)
 
         for stage in range(bits):
-            r = c - LAG * (stage + 1)
+            r = c - LAG * (stage + 1) - (REST if stage + 1 == bits else 0)
 
             @pl.when(jnp.logical_and(r >= 0, r < chunks))
             def _(r=r, stage=stage):
@@ -202,7 +203,7 @@
 
         return carry
 
-    lax.fori_loop(0, chunks + behind + LAG * bits, step, 0)
+    lax.fori_loop(0, chunks + behind + LAG * bits + REST, step, 0)
 
     def drain(t, carry):
         own_copy(t).wait_send()

time: 77.5 us -> 77.5 us (level)
  no operation moved by 1% of the time
where the time goes in v3:
time: 77.5 us; the launch traced here: 77.3 us
  Pallas kernels  73.6 us (95%)
  local copies, waits for them, and re-layouts  2.29 us (3%)
  other arithmetic  1.34 us (2%)
    pallas_call x1, Pallas kernels, shards(): pl.pallas_call(functools.partial(kernel, grid // 2, group, bits), out_sha...  73.6 us
    unnamed x4, local copies, waits for them, and re-layouts  2.29 us

profile of v3, /device:TPU:0, one launch (start us, length us, event | category | flops | bytes accessed | tf_op | source)
XLA Modules:
  0.0 77.3 jit_solution(17503839857426922962)
XLA Ops:
  0.0 0.0 copy-start
  0.0 1.6 %copy-done = f32[512,1024]{1,0:T(8,128)S(1)} copy-done((f32[512,1024]{1,0:T(8,128)S(1)}, f32[512,1024]{1,0:T(8,128)}, u32[]{:S(2)}) %copy-start) | copy-done | bytes 2097176
  1.6 0.0 copy-start.1
  1.6 0.7 copy-done.1
  2.3 73.6 %shard_map.28 = f32[256,1536]{1,0:T(8,128)S(1)} custom-call(f32[512,1024]{1,0:T(8,128)S(1)} %copy-done, s32[1536]{0:T(1024)S(1)} %copy-done.1), custom_call_target="tpu_custom_call" | custom-call | flops 8053063680 | bytes 4194304 | tf_op jit(solution)/shard_map/pallas_call | solution.py:234
  75.9 1.3 %mul.3 = f32[256,1536]{1,0:T(8,128)} multiply(f32[256,1536]{1,0:T(8,128)S(1)} %shard_map.28, f32[256,1536]{1,0:T(8,128)S(1)} %shard_map.28) | non-fusion elementwise | flops 393216 | bytes 4718592 | tf_op jit(solution)/shard_map/mul | solution.py:263
Async XLA Ops:
  0.0 1.6 %copy-start = (f32[512,1024]{1,0:T(8,128)S(1)}, f32[512,1024]{1,0:T(8,128)}, u32[]{:S(2)}) copy-start(f32[512,1024]{1,0:T(8,128)} %orb_ref.1) | copy-start | bytes 6291460
  1.6 0.7 copy-start.1
